TPU v7x, 512 devices: a whole 4x8x8 slice. The times are simulated.
512 devices in a mesh: aperture: 64 (over z, y_lo, x), tile: 8 (over y_hi, core).
Axes of the slice: x: 4, y: 8 (y_hi: 4, y_lo: 2; y = y_hi * 2 + y_lo), z: 8, core: 2. Of those that a mesh axis runs over, the one named last changes fastest.
Arguments:
- echoes: bfloat16 [2, 1024, 32768], P(None, 'aperture', 'tile'), may hold values from -6 to 6
- taps: bfloat16 [2, 4096], replicated, may hold values from -0.0625 to 0.0625
- steering: bfloat16 [2, 1024, 16], P(None, 'aperture'), may hold values from -1 to 1
- coefficients: float32 [2, 2, 2, 1024, 4], P(None, None, None, 'aperture'), may hold values from -2.5 to 2.5
- offsets: int32 [2, 2, 1024], P(None, None, 'aperture'), may hold values from 0 to 12
Outputs:
- image: float32 [2, 1024, 32768], P(None, 'aperture', 'tile')
Inputs may be any that keep to these rules, and one draw needn't show every extreme that they name: offsets + 3 is below 16.
All inputs are finite; a program needn't handle non-finite values.
Results may differ from a plain program's by a relative error of at most 0.0003.
Values may be sent and summed in bfloat16 or wider, within the bound.
A program may use at most 192 MiB of HBM per device.

v0:
```python
import jax
import jax.numpy as jnp
from jax import lax
from jax.experimental import pallas as pl
from jax.experimental.pallas import tpu as pltpu
from jax.sharding import PartitionSpec as P

BLOCK = 256
STEP = 1024
NB = 16
BAND = 4
MESH = pl.DeviceIdType.MESH
EXACT = lax.Precision.HIGHEST
NT = (((1,), (1,)), ((), ()))


def kernel(n_tile, x_ref, taps_ref, steer_ref, coef_ref, offs_ref, out_ref,
           gathered, toep, rows, acc, mats, views,
           x_send, x_recv, h_send, h_recv, p_send, p_recv):
    width = x_ref.shape[2]
    span = taps_ref.shape[1]
    chunks = width // STEP
    per = STEP // BLOCK
    rows_step = per * 64
    lags = span // STEP
    d = lax.axis_index("aperture")
    t = lax.axis_index("tile")
    x = lax.rem(d, 4)
    base = d - x
    mate = (d, base + x + 1 - 2 * lax.rem(x, 2), base + lax.rem(x + 2, 4), base + 3 - x)
    before = lax.rem(t + n_tile - 1, n_tile)
    after = lax.rem(t + 1, n_tile)

    barrier = pltpu.get_barrier_semaphore()
    for r in (1, 2, 3):
        pl.semaphore_signal(barrier, inc=1, device_id=(mate[r], t), device_id_type=MESH)
    for other in (before, after):
        pl.semaphore_signal(barrier, inc=1, device_id=(d, other), device_id_type=MESH)

    lane = lax.broadcasted_iota(jnp.int32, (NB, 128), 1)
    within = lax.rem(lane, 16).astype(jnp.float32)
    first = lax.rem(lane, 32) < 16
    eye = lax.broadcasted_iota(jnp.int32, (NB, NB), 0) == lax.broadcasted_iota(
        jnp.int32, (NB, NB), 1
    )

    def embedded(s, k):
        row = offs_ref[s][k : k + 1, :].astype(jnp.float32)
        start = jnp.sum(jnp.where(eye, row, 0.0), axis=1, keepdims=True)
        real = coef_ref[s, k, 0]
        imag = coef_ref[s, k, 1]
        top = jnp.zeros((NB, 128), jnp.float32)
        low = jnp.zeros((NB, 128), jnp.float32)
        for b in range(BAND):
            hit = within == start + float(b)
            re = real[:, b : b + 1]
            im = imag[:, b : b + 1]
            top += jnp.where(hit, jnp.where(first, re, -im), 0.0)
            low += jnp.where(hit, jnp.where(first, im, re), 0.0)
        return jnp.concatenate([top, low], axis=0)

    group = lax.broadcasted_iota(jnp.int32, (32, 128), 1) // 32
    mats[0] = jnp.where(group == 0, embedded(0, 0), jnp.where(group == 1, embedded(0, 1), 0.0))
    brow = lax.broadcasted_iota(jnp.int32, (NB, 128), 0)
    place0 = jnp.where((lax.rem(lane, 32) == brow) & (lane < 64), 1.0, 0.0).astype(jnp.bfloat16)
    place1 = jnp.where((lax.rem(lane, 32) == brow + 16) & (lane < 64), 1.0, 0.0).astype(
        jnp.bfloat16
    )
    s_re, s_im = steer_ref[0], steer_ref[1]

    def put(value, where):
        return jnp.dot(value, where, preferred_element_type=jnp.float32)

    views[0] = jnp.concatenate(
        [put(s_re, place0) + put(s_im, place1), put(s_re, place1) - put(s_im, place0)], axis=0
    )

    pl.semaphore_wait(barrier, 5)

    def remote(src, dst, send, recv, where):
        return pltpu.make_async_remote_copy(
            src_ref=src, dst_ref=dst, send_sem=send, recv_sem=recv,
            device_id=where, device_id_type=MESH,
        )

    small = [
        remote(views.at[0], views.at[r], p_send.at[r], p_recv.at[r], (mate[r], t))
        for r in (1, 2, 3)
    ]
    small.append(remote(mats.at[0], mats.at[1], p_send.at[0], p_recv.at[0], (mate[2], t)))

    def own(c, r):
        at = pl.ds(c * STEP, STEP)
        return remote(
            x_ref.at[:, :, at], gathered.at[r, :, :, at], x_send.at[r, c], x_recv.at[r, c],
            (mate[r], t),
        )

    def onward(c):
        at = pl.ds(c * STEP, STEP)
        came, goes = (1, 3) if c % 2 == 0 else (3, 1)
        return remote(
            gathered.at[came, :, :, at], gathered.at[2, :, :, at], x_send.at[2, c],
            x_recv.at[2, c], (mate[goes], t),
        )

    def halo(q):
        return remote(
            rows.at[pl.ds(q * rows_step, rows_step), :],
            rows.at[pl.ds((q + chunks) * rows_step, rows_step), :],
            h_send.at[q], h_recv.at[q], (d, before),
        )

    for copy in small:
        copy.start()
    for c in range(2):
        for r in (1, 3):
            own(c, r).start()

    def build(part, lo, hi):
        line = taps_ref[part : part + 1, :].astype(jnp.float32)
        padded = jnp.concatenate(
            [jnp.zeros((1, 128), jnp.float32), line, jnp.zeros((1, 256), jnp.float32)], axis=1
        )
        wide = jnp.broadcast_to(padded, (16, span + 384))
        for s in range(lo, hi):
            turned = pltpu.roll(wide, s * 16, 1, stride=1, stride_axis=0).astype(jnp.bfloat16)
            toep[part, pl.ds(s * 16, 16), :] = turned[:, 128:]
            toep[part, pl.ds(128 + s * 16, 16), :] = turned[:, : span + 256]

    def stage(q):
        for g in range(chunks):
            lag = q - g
            if lag < 0 or lag > lags:
                continue
            lo, hi = (0, 0) if lag == 0 else ((lag - 1) * per + 1, lag * per)
            left = jnp.concatenate(
                [rows[pl.ds((g * per + k) * 64, rows_step), :] for k in range(lo, hi + 1)], axis=1
            )
            for part in range(2):
                term = lax.dot_general(
                    left, toep[part, :, pl.ds(lo * BLOCK, (hi + 1 - lo) * BLOCK)], NT,
                    preferred_element_type=jnp.float32,
                )
                if lag == 0:
                    acc[part, pl.ds(g * rows_step, rows_step), :] = term
                else:
                    acc[part, pl.ds(g * rows_step, rows_step), :] += term

    def finish(g):
        for i in range(per):
            at = (g * per + i) * 64
            by_re = acc[0, pl.ds(at, 32), :] + acc[0, pl.ds(at + 32, 32), :]
            by_im = acc[1, pl.ds(at, 32), :] + acc[1, pl.ds(at + 32, 32), :]
            to = pl.ds((g * per + i) * BLOCK, BLOCK)
            out_ref[0, :, to] = by_re[:NB] - by_im[NB:]
            out_ref[1, :, to] = by_re[NB:] + by_im[:NB]

    build(0, 0, 4)

    last0 = embedded(1, 0)[:, :32]
    last1 = embedded(1, 1)[:, :32]
    for copy in small:
        copy.wait_recv()
    pair = (
        jnp.dot(last0, mats[0], precision=EXACT, preferred_element_type=jnp.float32),
        jnp.dot(last1, mats[1], precision=EXACT, preferred_element_type=jnp.float32),
    )
    view = views[...].reshape(128, 128)
    weights = jnp.zeros((32, 128), jnp.float32)
    for r in range(4):
        chosen = jnp.where(group == r % 2, pair[r // 2], 0.0)
        whole = lax.dot_general(
            chosen, view, NT, precision=EXACT, preferred_element_type=jnp.float32
        )
        weights = jnp.where(group == r, whole, weights)
    w_high = weights.astype(jnp.bfloat16)
    w_low = (weights - w_high.astype(jnp.float32)).astype(jnp.bfloat16)
    w_both = jnp.concatenate([w_high, w_low], axis=0)

    def pass_on(c):
        for r in (1, 3):
            own(c, r).wait_recv()
        onward(c).start()
        if c + 2 < chunks:
            for r in (1, 3):
                own(c + 2, r).start()

    def combine(c):
        onward(c).wait_recv()
        at = pl.ds(c * STEP, STEP)
        data = jnp.concatenate(
            [x_ref[:, :, at].reshape(32, STEP)]
            + [gathered[r, :, :, at].reshape(32, STEP) for r in (1, 2, 3)],
            axis=0,
        )
        both = jnp.dot(w_both, data, preferred_element_type=jnp.float32)
        value = both[:32] + both[32:]
        high = value.astype(jnp.bfloat16)
        low = (value - high.astype(jnp.float32)).astype(jnp.bfloat16)
        for i in range(per):
            lanes = slice(i * BLOCK, (i + 1) * BLOCK)
            rows[pl.ds((c * per + i) * 64, 32), :] = high[:, lanes]
            rows[pl.ds((c * per + i) * 64 + 32, 32), :] = low[:, lanes]

    pass_on(0)
    build(0, 4, 8)
    pass_on(1)
    build(1, 0, 8)
    for c in range(chunks):
        combine(c)

        @pl.when(t > 0)
        def _():
            halo(c).start()

        if c + 2 < chunks:
            pass_on(c + 2)
        stage(c)

    for q in range(chunks):
        @pl.when(t < n_tile - 1)
        def _():
            halo(q).wait_recv()

        @pl.when(t == n_tile - 1)
        def _():
            rows[pl.ds((q + chunks) * rows_step, rows_step), :] = jnp.zeros(
                (rows_step, BLOCK), jnp.bfloat16
            )

        stage(q + chunks)
        finish(q)

    for copy in small:
        copy.wait_send()
    for c in range(chunks):
        for r in (1, 3):
            own(c, r).wait_send()
        onward(c).wait_send()

        @pl.when(t > 0)
        def _():
            halo(c).wait_send()


def on_device(echoes, taps, steering, coefficients, offsets):
    width, span = echoes.shape[2], taps.shape[1]
    chunks = width // STEP
    blocks = (width + span) // BLOCK
    n_tile = lax.axis_size("tile")
    vmem = pl.BlockSpec(memory_space=pltpu.VMEM)
    dma = pltpu.SemaphoreType.DMA

    def body(*refs):
        kernel(n_tile, *refs)

    return pl.pallas_call(
        body,
        out_shape=jax.ShapeDtypeStruct((2, NB, width), jnp.float32),
        in_specs=[vmem] * 5,
        out_specs=vmem,
        scratch_shapes=[
            pltpu.VMEM((4, 2, NB, width), jnp.bfloat16),
            pltpu.VMEM((2, BLOCK, span + BLOCK), jnp.bfloat16),
            pltpu.VMEM((blocks * 64, BLOCK), jnp.bfloat16),
            pltpu.VMEM((2, width // BLOCK * 64, BLOCK), jnp.float32),
            pltpu.VMEM((2, 32, 128), jnp.float32),
            pltpu.VMEM((4, 32, 128), jnp.float32),
            dma((4, chunks)),
            dma((4, chunks)),
            dma((chunks,)),
            dma((chunks,)),
            dma((4,)),
            dma((4,)),
        ],
        compiler_params=pltpu.CompilerParams(
            collective_id=0, has_side_effects=True, vmem_limit_bytes=48 * 1024 * 1024
        ),
        cost_estimate=pl.CostEstimate(
            flops=2 * 1024 * 256 * 256 * 34 * 2, bytes_accessed=1 << 20, transcendentals=0
        ),
        name="backproject",
    )(echoes, taps, steering, coefficients, offsets)


def solution(mesh):
    in_specs = (
        P(None, "aperture", "tile"),
        P(),
        P(None, "aperture", None),
        P(None, None, None, "aperture", None),
        P(None, None, "aperture"),
    )
    out_specs = P(None, "aperture", "tile")
    return jax.shard_map(
        on_device, mesh=mesh, in_specs=in_specs, out_specs=out_specs, check_vma=False
    )
```

profile of v0, /device:TPU:1, one launch (start us, length us, event | category | flops | bytes accessed | tf_op | source)
XLA Modules:
  0.0 33.9 jit_solution(9853865988287970701)
XLA Ops:
  0.0 0.0 copy-start.3
  0.0 0.0 copy-start.2
  0.0 0.0 copy-start.1
  0.0 0.9 %copy.6.refs_3_ = f32[2,2,2,16,4]{4,3,2,1,0:T(8,128)S(1)} copy(f32[2,2,2,16,4]{3,4,2,1,0:T(4,128)} %param.8) | data formatting | bytes 4096 | tf_op args[3]
  0.9 0.0 copy-done.3
  0.9 0.0 copy-done.2
  0.9 0.0 copy-done.1
  0.9 0.0 copy-start
  0.9 0.9 %copy-done = bf16[2,16,4096]{2,1,0:T(8,128)(2,1)S(1)} copy-done((bf16[2,16,4096]{2,1,0:T(8,128)(2,1)S(1)}, bf16[2,16,4096]{2,1,0:T(8,128)(2,1)}, u32[]{:S(2)}) %copy-start) | copy-done | bytes 262168
  1.9 31.3 %backproject.1 = f32[2,16,4096]{2,1,0:T(8,128)S(1)} custom-call(bf16[2,16,4096]{2,1,0:T(8,128)(2,1)S(1)} %copy-done, bf16[2,4096]{1,0:T(2,128)(2,1)S(1)} %copy-done.1, bf16[2,16,16]{2,1,0:T(8,128)(2,1)S(1)} %copy-done.2, f32[2,2,2,16,4]{4,3,2,1,0:T(8,128)S(1)} %copy.6.refs_3_, s32[2,2,16]{2,1,0:T(2,128)S(1)} %copy-done.3), custom_call_target="tpu_custom_call" | custom-call | flops 9126805504 | bytes 1048576 | tf_op jit(solution)/shard_map/backproject/pallas_call | solution.py:258
  33.2 0.8 %copy.8 = f32[2,16,4096]{2,1,0:T(8,128)} copy(f32[2,16,4096]{2,1,0:T(8,128)S(1)} %backproject.1) | data formatting | bytes 1048576
Async XLA Ops:
  0.0 0.9 %copy-start.3 = (s32[2,2,16]{2,1,0:T(2,128)S(1)}, s32[2,2,16]{2,1,0:T(2,128)}, u32[]{:S(2)}) copy-start(s32[2,2,16]{2,1,0:T(2,128)} %refs_4_.1) | copy-start | bytes 772
  0.0 0.9 %copy-start.2 = (bf16[2,16,16]{2,1,0:T(8,128)(2,1)S(1)}, bf16[2,16,16]{2,1,0:T(8,128)(2,1)}, u32[]{:S(2)}) copy-start(bf16[2,16,16]{2,1,0:T(8,128)(2,1)} %refs_2_.1) | copy-start | bytes 3076
  0.0 0.9 %copy-start.1 = (bf16[2,4096]{1,0:T(2,128)(2,1)S(1)}, bf16[2,4096]{1,0:T(2,128)(2,1)}, u32[]{:S(2)}) copy-start(bf16[2,4096]{1,0:T(2,128)(2,1)} %refs_1_.1) | copy-start | bytes 49156
  0.9 1.0 %copy-start = (bf16[2,16,4096]{2,1,0:T(8,128)(2,1)S(1)}, bf16[2,16,4096]{2,1,0:T(8,128)(2,1)}, u32[]{:S(2)}) copy-start(bf16[2,16,4096]{2,1,0:T(8,128)(2,1)} %refs_0_.1) | copy-start | bytes 786436
where the time goes:
time: 34.1 us; the launch traced here: 33.9 us
  Pallas kernels  31.3 us (92%)
  local copies, waits for them, and re-layouts  2.62 us (8%)
    pallas_call x1, Pallas kernels, on_device(): pl.pallas_call(body, out_shape=jax.ShapeDtypeStruct((2, NB, width), jnp.f...  31.3 us
    unnamed x10, local copies, waits for them, and re-layouts  2.62 us

commit v1 on v0

v1 whole, which is shorter than its diff:
```python
import jax
import jax.numpy as jnp
from jax import lax
from jax.experimental import pallas as pl
from jax.experimental.pallas import tpu as pltpu
from jax.sharding import PartitionSpec as P

BLOCK = 256
STEP = 512
VMEM = 48 * 1024 * 1024
LEAD = 3
LEVELS = 32767.0
WINDOW = 4
GROUP = 1024
NB = 16
BAND = 4
MESH = pl.DeviceIdType.MESH
EXACT = lax.Precision.HIGHEST
NT = (((1,), (1,)), ((), ()))


def kernel(n_tile, x_ref, taps_hbm, steer_hbm, coef_hbm, offs_hbm, out_ref,
           gathered, toep, rows, acc, mats, views, coded,
           taps_ref, steer_ref, coef_ref, offs_ref,
           x_send, x_recv, h_send, h_recv, p_send, p_recv, l_sem):
    width = x_ref.shape[2]
    span = taps_ref.shape[1]
    chunks = width // STEP
    step_rows = STEP // BLOCK * 64
    groups = width // GROUP
    per = GROUP // BLOCK
    group_rows = per * 64
    lags = span // GROUP
    ratio = GROUP // STEP
    d = lax.axis_index("aperture")
    t = lax.axis_index("tile")
    x = lax.rem(d, 4)
    base = d - x
    mate = (d, base + x + 1 - 2 * lax.rem(x, 2), base + lax.rem(x + 2, 4), base + 3 - x)
    before = lax.rem(t + n_tile - 1, n_tile)
    after = lax.rem(t + 1, n_tile)

    local = [
        pltpu.make_async_copy(src, dst, l_sem.at[k])
        for k, (src, dst) in enumerate(
            [(steer_hbm, steer_ref), (coef_hbm, coef_ref), (offs_hbm, offs_ref),
             (taps_hbm, taps_ref), (x_ref, gathered.at[0])]
        )
    ]
    barrier = pltpu.get_barrier_semaphore()
    for r in (1, 2, 3):
        pl.semaphore_signal(barrier, inc=1, device_id=(mate[r], t), device_id_type=MESH)
    for other in (before, after):
        pl.semaphore_signal(barrier, inc=1, device_id=(d, other), device_id_type=MESH)

    for copy in local:
        copy.start()
    pl.semaphore_wait(barrier, 5)

    def remote(src, dst, send, recv, where):
        return pltpu.make_async_remote_copy(
            src_ref=src, dst_ref=dst, send_sem=send, recv_sem=recv,
            device_id=where, device_id_type=MESH,
        )

    small = [
        remote(views.at[0], views.at[r], p_send.at[r], p_recv.at[r], (mate[r], t))
        for r in (1, 2, 3)
    ]
    small.append(remote(mats.at[0], mats.at[1], p_send.at[0], p_recv.at[0], (mate[2], t)))

    def own(c, r):
        at = pl.ds(c * STEP, STEP)
        return remote(
            x_ref.at[:, :, at], gathered.at[r, :, :, at], x_send.at[r, c], x_recv.at[r, c],
            (mate[r], t),
        )

    def onward(c):
        at = pl.ds(c * STEP, STEP)
        came, goes = (1, 3) if c % 2 == 0 else (3, 1)
        return remote(
            gathered.at[came, :, :, at], gathered.at[2, :, :, at], x_send.at[2, c],
            x_recv.at[2, c], (mate[goes], t),
        )

    def halo(q):
        return remote(
            coded.at[0, q], coded.at[1, q], h_send.at[q], h_recv.at[q], (d, before),
        )

    for c in range(WINDOW):
        for r in (1, 3):
            own(c, r).start()
    for copy in local[:4]:
        copy.wait()

    lane = lax.broadcasted_iota(jnp.int32, (NB, 128), 1)
    beam = lax.broadcasted_iota(jnp.int32, (NB, 128), 0)
    first = lax.rem(lane, 32) < 16
    group = lax.broadcasted_iota(jnp.int32, (32, 128), 1) // 32
    repeat = jnp.where(lax.rem(lane, 16) == beam, 1.0, 0.0)

    def flipped(s, k):
        offs = offs_ref[s].astype(jnp.float32)
        start = jnp.dot(offs, repeat, precision=EXACT, preferred_element_type=jnp.float32)
        real, imag = (
            jnp.dot(coef_ref[s, k, part], repeat, precision=EXACT, preferred_element_type=jnp.float32)
            for part in range(2)
        )
        top = jnp.zeros((NB, 128), jnp.float32)
        low = jnp.zeros((NB, 128), jnp.float32)
        for b in range(BAND):
            hit = beam.astype(jnp.float32) == start[k : k + 1] + float(b)
            re, im = real[b : b + 1], imag[b : b + 1]
            top += jnp.where(hit, jnp.where(first, re, im), 0.0)
            low += jnp.where(hit, jnp.where(first, -im, re), 0.0)
        return jnp.concatenate([top, low], axis=0)


    mats[0] = jnp.where(lax.rem(group, 2) == 0, flipped(0, 0), flipped(0, 1))
    place0 = jnp.where(lane == beam, 1.0, 0.0).astype(jnp.bfloat16)
    place1 = jnp.where(lane == beam + 16, 1.0, 0.0).astype(jnp.bfloat16)
    s_re, s_im = steer_ref[0], steer_ref[1]

    def put(value, where):
        return jnp.dot(value, where, preferred_element_type=jnp.float32)

    views[0] = jnp.concatenate(
        [put(s_re, place0) + put(s_im, place1), put(s_re, place1) - put(s_im, place0)], axis=0
    )
    for copy in small:
        copy.start()

    def build(part, lo, hi):
        line = taps_ref[part : part + 1, :].astype(jnp.float32)
        padded = jnp.concatenate(
            [jnp.zeros((1, 128), jnp.float32), line, jnp.zeros((1, 256), jnp.float32)], axis=1
        )
        wide = jnp.broadcast_to(padded, (16, span + 384))
        for s in range(lo, hi):
            turned = pltpu.roll(wide, s * 16, 1, stride=1, stride_axis=0).astype(jnp.bfloat16)
            toep[part, pl.ds(s * 16, 16), :] = turned[:, 128:]
            toep[part, pl.ds(128 + s * 16, 16), :] = turned[:, : span + 256]

    def stage(q):
        for g in range(groups):
            lag = q - g
            if lag < 0 or lag > lags:
                continue
            lo, hi = (0, 0) if lag == 0 else ((lag - 1) * per + 1, lag * per)
            left = jnp.concatenate(
                [rows[pl.ds((g * per + k) * 64, group_rows), :] for k in range(lo, hi + 1)], axis=1
            )
            for part in range(2):
                term = lax.dot_general(
                    left, toep[part, :, pl.ds(lo * BLOCK, (hi + 1 - lo) * BLOCK)], NT,
                    preferred_element_type=jnp.float32,
                )
                if lag == 0:
                    acc[part, pl.ds(g * group_rows, group_rows), :] = term
                else:
                    acc[part, pl.ds(g * group_rows, group_rows), :] += term

    def finish(g):
        for i in range(per):
            at = (g * per + i) * 64
            by_re = acc[0, pl.ds(at, 32), :] + acc[0, pl.ds(at + 32, 32), :]
            by_im = acc[1, pl.ds(at, 32), :] + acc[1, pl.ds(at + 32, 32), :]
            to = pl.ds((g * per + i) * BLOCK, BLOCK)
            out_ref[0, :, to] = by_re[:NB] - by_im[NB:]
            out_ref[1, :, to] = by_re[NB:] + by_im[:NB]

    def pass_on(c):
        for r in (1, 3):
            own(c, r).wait_recv()
        onward(c).start()
        if c + WINDOW < chunks:
            for r in (1, 3):
                own(c + WINDOW, r).start()

    def keep(at, value):
        high = value.astype(jnp.bfloat16)
        rows[pl.ds(at, 32), :] = high
        rows[pl.ds(at + 32, 32), :] = (value - high.astype(jnp.float32)).astype(jnp.bfloat16)

    def combine(c):
        onward(c).wait_recv()
        at = pl.ds(c * STEP, STEP)
        data = gathered[:, :, :, at].reshape(128, STEP)
        both = jnp.dot(w_both, data, preferred_element_type=jnp.float32)
        value = both[:32] + both[32:]
        for i in range(STEP // BLOCK):
            part = value[:, i * BLOCK : (i + 1) * BLOCK]
            keep(c * step_rows + i * 64, part)
            peak = jnp.maximum(jnp.max(jnp.abs(part), axis=1, keepdims=True), 1e-30)
            power = jnp.ceil(16.0 * jnp.log2(peak / LEVELS))
            level = jnp.round(part / jnp.exp2(power / 16.0))
            level = jnp.clip(level, -LEVELS, LEVELS)
            coded[0, c, :, pl.ds(i * BLOCK, BLOCK)] = level.astype(jnp.int32).astype(jnp.int16)
            coded[0, c, :, pl.ds(STEP + i * 128, 128)] = jnp.broadcast_to(
                power.astype(jnp.int32), (32, 128)
            ).astype(jnp.int16)

    def decode(q):
        for i in range(STEP // BLOCK):
            level = coded[1, q, :, pl.ds(i * BLOCK, BLOCK)].astype(jnp.int32).astype(jnp.float32)
            power = coded[1, q, :, pl.ds(STEP + i * 128, 128)].astype(jnp.int32)
            scale = jnp.exp2(power.astype(jnp.float32)[:, :1] / 16.0)
            keep((q + chunks) * step_rows + i * 64, level * scale)

    def make_weights():
        last = [jnp.concatenate([flipped(1, k)] * 4, axis=0) for k in range(2)]
        for copy in small:
            copy.wait_recv()
        columns = []
        for k in range(2):
            view = views[pl.ds(2 * k, 2)].reshape(64, 128)
            once = jnp.dot(
                view[:, :32], mats[k], precision=EXACT, preferred_element_type=jnp.float32
            )
            once = jnp.concatenate(
                [jnp.where(group == 0, once[:32], 0.0), jnp.where(group == 1, once[32:], 0.0)], axis=0
            )
            columns.append(
                jnp.dot(once, last[k], precision=EXACT, preferred_element_type=jnp.float32)
            )
        weights = jnp.concatenate(columns, axis=0).T[:32]
        w_high = weights.astype(jnp.bfloat16)
        w_low = (weights - w_high.astype(jnp.float32)).astype(jnp.bfloat16)
        w_both = jnp.concatenate([w_high, w_low], axis=0)
        return w_both

    todo = [(part, lo) for part in range(2) for lo in range(8)]

    def some(count):
        for _ in range(min(count, len(todo))):
            part, lo = todo.pop(0)
            build(part, lo, lo + 1)

    some(2)
    for c in range(LEAD):
        pass_on(c)
        some(3)
    w_both = make_weights()
    local[4].wait()
    done = 0
    for c in range(chunks):
        if c + LEAD < chunks:
            pass_on(c + LEAD)
        combine(c)

        @pl.when(t > 0)
        def _():
            halo(c).start()

        some(3)
        if not todo and (done + 1) * ratio <= c + 1:
            stage(done)
            done += 1
    for q in range(done, groups):
        stage(q)

    for q in range(groups):
        @pl.when(t < n_tile - 1)
        def _():
            for c in range(q * ratio, (q + 1) * ratio):
                halo(c).wait_recv()
                decode(c)

        @pl.when(t == n_tile - 1)
        def _():
            rows[pl.ds((q + groups) * group_rows, group_rows), :] = jnp.zeros(
                (group_rows, BLOCK), jnp.bfloat16
            )

        stage(q + groups)
        finish(q)

    for copy in small:
        copy.wait_send()
    for c in range(chunks):
        for r in (1, 3):
            own(c, r).wait_send()
        onward(c).wait_send()

        @pl.when(t > 0)
        def _():
            halo(c).wait_send()


def on_device(echoes, taps, steering, coefficients, offsets):
    width, span = echoes.shape[2], taps.shape[1]
    chunks = width // STEP
    blocks = (width + span) // BLOCK
    n_tile = lax.axis_size("tile")
    vmem = pl.BlockSpec(memory_space=pltpu.VMEM)
    dma = pltpu.SemaphoreType.DMA

    def body(*refs):
        kernel(n_tile, *refs)

    return pl.pallas_call(
        body,
        out_shape=jax.ShapeDtypeStruct((2, NB, width), jnp.float32),
        in_specs=[pl.BlockSpec(memory_space=pltpu.HBM)] * 5,
        out_specs=vmem,
        scratch_shapes=[
            pltpu.VMEM((4, 2, NB, width), jnp.bfloat16),
            pltpu.VMEM((2, BLOCK, span + BLOCK), jnp.bfloat16),
            pltpu.VMEM((blocks * 64, BLOCK), jnp.bfloat16),
            pltpu.VMEM((2, width // BLOCK * 64, BLOCK), jnp.float32),
            pltpu.VMEM((2, 32, 128), jnp.float32),
            pltpu.VMEM((4, 32, 128), jnp.float32),
            pltpu.VMEM((2, chunks, 32, STEP + STEP // BLOCK * 128), jnp.int16),
            pltpu.VMEM(taps.shape, taps.dtype),
            pltpu.VMEM(steering.shape, steering.dtype),
            pltpu.VMEM((2, 2, 2, BAND, NB), jnp.float32),
            pltpu.VMEM(offsets.shape, offsets.dtype),
            dma((4, chunks)),
            dma((4, chunks)),
            dma((chunks,)),
            dma((chunks,)),
            dma((4,)),
            dma((4,)),
            dma((5,)),
        ],
        compiler_params=pltpu.CompilerParams(
            collective_id=0, has_side_effects=True, vmem_limit_bytes=VMEM
        ),
        cost_estimate=pl.CostEstimate(
            flops=2 * 1024 * 256 * 256 * 34 * 2, bytes_accessed=1 << 20, transcendentals=0
        ),
        name="backproject",
    )(
        *(
            pltpu.with_memory_space_constraint(value, pltpu.HBM)
            for value in (echoes, taps, steering, jnp.swapaxes(coefficients, 3, 4), offsets)
        )
    )


def solution(mesh):
    in_specs = (
        P(None, "aperture", "tile"),
        P(),
        P(None, "aperture", None),
        P(None, None, None, "aperture", None),
        P(None, None, "aperture"),
    )
    out_specs = P(None, "aperture", "tile")
    return jax.shard_map(
        on_device, mesh=mesh, in_specs=in_specs, out_specs=out_specs, check_vma=False
    )
```

time: 34.1 us -> 29 us (0.85)
  the two profiles are of different devices: /device:TPU:1 before, /device:TPU:2 now
where the time goes in v1:
time: 29 us; the launch traced here: 28.8 us
  Pallas kernels  28 us (97%)
  local copies, waits for them, and re-layouts  0.8 us (3%)
    pallas_call x1, Pallas kernels, on_device(): pl.pallas_call(body, out_shape=jax.ShapeDtypeStruct((2, NB, width), jnp.f...  28 us
    unnamed x1, local copies, waits for them, and re-layouts  0.8 us

profile of v1, /device:TPU:2, one launch (start us, length us, event | category | flops | bytes accessed | tf_op | source)
XLA Modules:
  0.0 28.8 jit_solution(11492488492443090587)
XLA Ops:
  0.0 28.0 %backproject.1 = f32[2,16,4096]{2,1,0:T(8,128)S(1)} custom-call(bf16[2,16,4096]{2,1,0:T(8,128)(2,1)} %refs_0_.1, bf16[2,4096]{1,0:T(2,128)(2,1)} %refs_1_.1, bf16[2,16,16]{2,1,0:T(8,128)(2,1)} %refs_2_.1, f32[2,2,2,4,16]{4,3,2,1,0:T(4,128)} %bitcast.1, s32[2,2,16]{2,1,0:T(2,128)} %refs_4_.1), custom_call_target="tpu_custom_call" | custom-call | flops 9126805504 | bytes 1048576 | tf_op jit(solution)/shard_map/backproject/pallas_call | solution.py:303
  28.0 0.8 %copy.7 = f32[2,16,4096]{2,1,0:T(8,128)} copy(f32[2,16,4096]{2,1,0:T(8,128)S(1)} %backproject.1) | data formatting | bytes 1048576
